TPU v7x, 32 devices: a whole 2x2x4 slice. The times are simulated.
32 devices in a mesh: groups: 2 (over y), expert: 4 (over z), attn: 2 (over x), tp: 2 (over core).
Axes of the slice: x: 2, y: 2, z: 4, core: 2. Of those that a mesh axis runs over, the one named last changes fastest.
Arguments:
- queries: bfloat16 [16, 64, 128], P(('groups', 'expert', 'attn'), 'tp'), parts along dimension 0, may hold values from -8 to 8
- new_keys: bfloat16 [16, 4, 128], P(('groups', 'expert', 'attn'), 'tp'), parts along dimension 0, may hold values from -6 to 6
- new_values: bfloat16 [16, 4, 128], P(('groups', 'expert', 'attn'), 'tp'), parts along dimension 0, may hold values from -6 to 6
- kv_cache: bfloat16 [64, 64, 2, 4, 128], P(('groups', 'expert', 'attn'), None, None, 'tp'), parts along dimension 0, may hold values from -8 to 8
- block_tables: int32 [16, 4], P(('groups', 'expert', 'attn')), parts along dimension 0, may hold values from 0 to 3, as said below
- cache_lengths: int32 [16], P(('groups', 'expert', 'attn')), parts along dimension 0, may hold values from 3 to 256, as said below
- tokens: bfloat16 [1024, 2048], P(('groups', 'expert', 'attn', 'tp')), parts along dimension 0, may hold values from -200 to 200
- gain: float32 [2048], replicated, may hold values from 0.5 to 1.5
- expert_ids: int32 [1024, 8], P(('groups', 'expert', 'attn', 'tp')), parts along dimension 0, may hold values from 0 to 15, all different within a row; in each aligned block of 32 rows (0 to 31, 32 to 63, ...) at most 17 rows name the same one
- gate_weights: float32 [1024, 8], P(('groups', 'expert', 'attn', 'tp')), parts along dimension 0, may hold values from 0.05 to 1
- w_in: bfloat16 [16, 2, 1536, 2048], P(('expert', 'attn', 'tp')), may hold values from -0.125 to 0.125
- w_out: bfloat16 [16, 1536, 2048], P(('expert', 'attn', 'tp')), may hold values from -0.15625 to 0.15625
Outputs:
- attn_out: bfloat16 [16, 64, 128], P(('groups', 'expert', 'attn'), 'tp'), parts along dimension 0
- moe_out: bfloat16 [1024, 2048], P(('groups', 'expert', 'attn', 'tp')), parts along dimension 0
There are 2 independent parts, one for each index of `groups`. A program takes and returns all parts, laid end to end along the dimension named above; an argument that names none is the same for every part. Nothing has to cross between parts.
Inputs may be any that keep to these rules, and one draw needn't show every extreme that they name: `block_tables`: within each attention group of 1 rows the entries are the page numbers of that group, each once. `cache_lengths`: some row holds exactly 256 cached tokens. `expert_ids`: each row names 8 different experts; within each aligned block of 32 rows (the rows of one device) no expert is named more than 17 times, and in some block some expert exactly 17 times; every expert is named somewhere.
All inputs are finite; a program needn't handle non-finite values.
Results may differ from a plain program's by a relative error of at most 0.0071.
Values may be sent and summed in bfloat16 or wider, within the bound.
A program may use at most 64 MiB of HBM per device.

v0:
```python
import jax
import jax.numpy as jnp
from jax import lax
from jax.sharding import PartitionSpec as P

TOP = 8
EXP_RANK = 4


epsilon = 1e-06


def attend(queries, new_keys, new_values, kv_cache, block_tables, cache_lengths):
    rows, heads, size = queries.shape
    kv_heads = new_keys.shape[1]
    grouped = queries.reshape(rows, kv_heads, heads // kv_heads, size)
    pages = kv_cache[block_tables]
    span = pages.shape[1] * pages.shape[2]
    pages = pages.reshape(rows, span, 2, kv_heads, size)
    scale = size ** (-0.5)
    scores = (
        jnp.einsum("rkgd,rlkd->rkgl", grouped, pages[:, :, 0], preferred_element_type=jnp.float32)
        * scale
    )
    inside = jnp.arange(span, dtype=jnp.int32)[None, :] < cache_lengths[:, None]
    scores = jnp.where(inside[:, None, None, :], scores, -jnp.inf)
    own = jnp.einsum("rkgd,rkd->rkg", grouped, new_keys, preferred_element_type=jnp.float32) * scale
    top = jnp.maximum(jnp.max(scores, axis=3), own)
    weights = jnp.exp(scores - top[..., None])
    own_weight = jnp.exp(own - top)
    total = jnp.sum(weights, axis=3) + own_weight
    probs = (weights / total[..., None]).astype(jnp.bfloat16)
    own_prob = (own_weight / total).astype(jnp.bfloat16)
    mixed = jnp.einsum("rkgl,rlkd->rkgd", probs, pages[:, :, 1], preferred_element_type=jnp.float32)
    mixed = (
        mixed
        + own_prob.astype(jnp.float32)[..., None] * new_values.astype(jnp.float32)[:, :, None, :]
    )
    return mixed.astype(jnp.bfloat16).reshape(rows, heads, size)


def expert_part(rows_in, weights_in, weights_out):
    both = jnp.einsum("nd,gud->gnu", rows_in, weights_in, preferred_element_type=jnp.float32)
    hidden = (jax.nn.silu(both[0]) * both[1]).astype(jnp.bfloat16)
    return jnp.dot(hidden, weights_out, preferred_element_type=jnp.float32).astype(jnp.bfloat16)


def per_device(
    queries,
    new_keys,
    new_values,
    kv_cache,
    block_tables,
    cache_lengths,
    tokens,
    gain,
    expert_ids,
    gate_weights,
    w_in,
    w_out,
):
    attn_out = attend(queries, new_keys, new_values, kv_cache, block_tables, cache_lengths)
    rows, width = tokens.shape
    ranks = lax.axis_size("expert")
    peers = lax.axis_size(("attn", "tp"))
    slices = peers // EXP_RANK
    experts = EXP_RANK * ranks
    most = max(2, rows * TOP // experts + 1)
    floats = tokens.astype(jnp.float32)
    normed = (
        floats * lax.rsqrt(jnp.mean(floats * floats, axis=1, keepdims=True) + epsilon) * gain
    ).astype(jnp.bfloat16)
    chosen = expert_ids.reshape(-1)
    onehot = (chosen[:, None] == jnp.arange(experts, dtype=jnp.int32)[None, :]).astype(jnp.int32)
    earlier = jnp.cumsum(onehot, axis=0) - onehot
    targets = chosen * most + jnp.sum(earlier * onehot, axis=1)
    picks = (jnp.arange(experts * most, dtype=jnp.int32)[:, None] == targets[None, :]).astype(
        jnp.int32
    )
    picks = jnp.sum(picks.reshape(experts * most, rows, TOP), axis=2).astype(jnp.bfloat16)
    buckets = jnp.dot(picks, normed, preferred_element_type=jnp.float32).astype(jnp.bfloat16)
    buckets = buckets.reshape(experts, most, width)
    grouped = buckets.reshape(ranks, EXP_RANK, most, width)
    copies = jnp.repeat(grouped, slices, axis=1)
    in_rank = lax.all_to_all(copies, ("attn", "tp"), split_axis=1, concat_axis=1, tiled=True)
    arrived = lax.all_to_all(in_rank, "expert", split_axis=0, concat_axis=0, tiled=True)
    partial_rows = expert_part(arrived.reshape(-1, width), w_in[0], w_out[0])
    partial_rows = partial_rows.reshape(ranks, peers, most, width)
    returned = lax.all_to_all(partial_rows, "expert", split_axis=0, concat_axis=0, tiled=True)
    gathered = lax.all_to_all(returned, ("attn", "tp"), split_axis=1, concat_axis=1, tiled=True)
    summed = jnp.sum(
        gathered.reshape(ranks, EXP_RANK, slices, most, width).astype(jnp.float32), axis=2
    )
    home = summed.astype(jnp.bfloat16).reshape(experts, most, width)
    flat_home = home.reshape(experts * most, width)
    shares = gate_weights / jnp.sum(gate_weights, axis=1, keepdims=True)
    placed = targets.reshape(rows, TOP)
    mixed = jnp.zeros((rows, width), jnp.float32)
    for column in range(TOP):
        mixed = mixed + shares[:, column : column + 1] * flat_home[placed[:, column]].astype(
            jnp.float32
        )
    return (attn_out, mixed.astype(jnp.bfloat16))


def solution(mesh):
    return jax.shard_map(
        per_device,
        mesh=mesh,
        in_specs=(
            P(("groups", "expert", "attn"), "tp", None),
            P(("groups", "expert", "attn"), "tp", None),
            P(("groups", "expert", "attn"), "tp", None),
            P(("groups", "expert", "attn"), None, None, "tp", None),
            P(("groups", "expert", "attn"), None),
            P(("groups", "expert", "attn")),
            P(("groups", "expert", "attn", "tp"), None),
            P(),
            P(("groups", "expert", "attn", "tp"), None),
            P(("groups", "expert", "attn", "tp"), None),
            P(("expert", "attn", "tp"), None, None, None),
            P(("expert", "attn", "tp"), None, None),
        ),
        out_specs=(
            P(("groups", "expert", "attn"), "tp", None),
            P(("groups", "expert", "attn", "tp"), None),
        ),
        check_vma=False,
    )
```

profile of v0, /device:TPU:0, one launch (start us, length us, event | category | flops | bytes accessed | tf_op | source)
XLA Modules:
  0.0 133.0 jit_solution(6342301208833457269)
XLA Ops:
  0.6 0.0 copy-start
  0.6 0.8 copy.38
  1.4 0.1 eq.44
  1.5 0.1 eq.40
  1.6 0.6 reduce-window.6
  2.2 0.2 slice_reduce_fusion
  2.5 0.1 fusion.34
  2.6 0.1 reduce_sum.54
  2.7 0.2 convert_reduce_fusion
  2.9 1.0 fusion.16
  3.9 1.4 %convolution_convert_fusion = bf16[272,2048]{1,0:T(8,128)(2,1)S(1)} fusion(bf16[32,2048]{1,0:T(8,128)(2,1)} %param.18, f32[2048]{0:T(1024)} %param.19, f32[32]{0:T(128)S(1)} %add_rsqrt_fusion, s32[272,32]{0,1:T(8,128)S(1)} %convert_reduce_fusion), kind=kOutput, calls=%fused_computation.14 | convolution fusion | flops 36479488 | bytes 1288320 | tf_op jit(solution)/shard_map/dot_general | solution.py:81
  5.3 0.5 reshape_broadcast_in_dim_reshape_reshape.3
  5.8 0.9 copy.42
  6.7 19.2 %all_to_all.20 = bf16[4,4,17,2048]{3,0,2,1:T(4,128)(2,1)S(1)} all-to-all(bf16[4,4,17,2048]{3,0,2,1:T(4,128)(2,1)S(1)} %copy.42), channel_id=1, replica_groups=mesh['groups'=2,'expert'=4,'attn'=2,'tp'=2] {'attn','tp'}, dimensions={1} | all-to-all | bytes 2228224 | tf_op jit(solution)/shard_map/all_to_all | solution.py:85
  25.9 1.9 %copy.43 = bf16[4,4,17,2048]{3,1,2,0:T(4,128)(2,1)} copy(bf16[4,4,17,2048]{3,0,2,1:T(4,128)(2,1)S(1)} %all_to_all.20) | data formatting | bytes 2228224 | tf_op jit(solution)/shard_map/all_to_all | solution.py:85
  27.7 0.0 copy-start.3
  27.7 5.0 %all-to-all-start.1 = ((bf16[4,4,17,2048]{3,1,2,0:T(4,128)(2,1)}), bf16[4,4,17,2048]{3,1,2,0:T(4,128)(2,1)S(1)}, u32[]{:S(2)}, u32[]{:S(2)}) async-start(bf16[4,4,17,2048]{3,1,2,0:T(4,128)(2,1)} %copy.43), calls=%async_computation.1 | async-start | bytes 2228224 | tf_op jit(solution)/shard_map/all_to_all | solution.py:86
  32.7 0.0 copy-done.3
  32.7 0.0 copy-done
  32.8 1.1 gather_fusion
  34.5 25.2 %all-to-all-done.1 = bf16[4,4,17,2048]{3,1,2,0:T(4,128)(2,1)S(1)} async-done(((bf16[4,4,17,2048]{3,1,2,0:T(4,128)(2,1)}), bf16[4,4,17,2048]{3,1,2,0:T(4,128)(2,1)S(1)}, u32[]{:S(2)}, u32[]{:S(2)}) %all-to-all-start.1) | async-done | bytes 1114144 | tf_op jit(solution)/shard_map/all_to_all | solution.py:86
  59.8 0.7 copy.44
  60.4 0.5 reshape.230
  60.9 6.7 %fusion.4 = f32[2,272,1536]{2,1,0:T(8,128)S(1)} fusion(bf16[272,2048,1]{1,0,2:T(8,128)(2,1)S(1)} %reshape.230, bf16[1,2,1536,2048]{3,2,1,0:T(8,128)(2,1)} %param.22), kind=kOutput, calls=%fused_computation.13 | convolution fusion | flops 3422552064 | bytes 17039360 | tf_op jit(solution)/shard_map/nd,gud->gnu/dot_general | solution.py:43
  67.6 4.7 %fusion.7 = bf16[272,2048]{1,0:T(8,128)(2,1)S(1)} fusion(bf16[1,1536,2048]{2,1,0:T(8,128)(2,1)} %param.23, f32[2,272,1536]{2,1,0:T(8,128)S(1)} %fusion.4), kind=kOutput, calls=%fused_computation.15 | convolution fusion | flops 1714339840 | bytes 10747904 | tf_op jit(solution)/shard_map/dot_general | solution.py:45
  72.4 0.5 reshape.152
  72.8 1.9 %copy.45 = bf16[4,4,17,2048]{3,1,2,0:T(4,128)(2,1)} copy(bf16[4,4,17,2048]{3,2,1,0:T(8,128)(2,1)S(1)} %reshape.152) | data formatting | bytes 2228224 | tf_op jit(solution)/shard_map/reshape | solution.py:88
  74.7 0.0 copy-start.2
  74.7 0.0 copy-start.4
  74.7 0.0 copy-start.5
  74.7 3.7 %all-to-all-start.2 = ((bf16[4,4,17,2048]{3,1,2,0:T(4,128)(2,1)}), bf16[4,4,17,2048]{3,1,2,0:T(4,128)(2,1)S(1)}, u32[]{:S(2)}, u32[]{:S(2)}) async-start(bf16[4,4,17,2048]{3,1,2,0:T(4,128)(2,1)} %copy.45), calls=%async_computation.2 | async-start | bytes 2228224 | tf_op jit(solution)/shard_map/all_to_all | solution.py:89
  78.4 0.3 fusion.24
  78.7 0.0 copy-done.2
  78.7 0.0 copy-done.4
  78.7 0.1 fusion.38
  78.9 0.2 fusion.44
  79.1 0.2 fusion.22
  79.3 0.0 copy-done.5
  79.3 25.7 %all-to-all-done.2 = bf16[4,4,17,2048]{3,1,2,0:T(4,128)(2,1)S(1)} async-done(((bf16[4,4,17,2048]{3,1,2,0:T(4,128)(2,1)}), bf16[4,4,17,2048]{3,1,2,0:T(4,128)(2,1)S(1)}, u32[]{:S(2)}, u32[]{:S(2)}) %all-to-all-start.2) | async-done | bytes 1114144 | tf_op jit(solution)/shard_map/all_to_all | solution.py:89
  105.0 1.9 %copy.46 = bf16[4,4,17,2048]{3,0,2,1:T(4,128)(2,1)} copy(bf16[4,4,17,2048]{3,1,2,0:T(4,128)(2,1)S(1)} %all-to-all-done.2) | data formatting | bytes 2228224 | tf_op jit(solution)/shard_map/all_to_all | solution.py:89
  106.8 0.0 copy-start.1
  106.8 3.7 %all-to-all-start.3 = ((bf16[4,4,17,2048]{3,0,2,1:T(4,128)(2,1)}), bf16[4,4,17,2048]{3,0,2,1:T(4,128)(2,1)S(1)}, u32[]{:S(2)}, u32[]{:S(2)}) async-start(bf16[4,4,17,2048]{3,0,2,1:T(4,128)(2,1)} %copy.46), calls=%async_computation.3 | async-start | bytes 2228224 | tf_op jit(solution)/shard_map/all_to_all | solution.py:90
  110.5 0.0 copy-done.1
  110.6 0.8 fusion.13
  111.4 14.2 %all-to-all-done.3 = bf16[4,4,17,2048]{3,0,2,1:T(4,128)(2,1)S(1)} async-done(((bf16[4,4,17,2048]{3,0,2,1:T(4,128)(2,1)}), bf16[4,4,17,2048]{3,0,2,1:T(4,128)(2,1)S(1)}, u32[]{:S(2)}, u32[]{:S(2)}) %all-to-all-start.3) | async-done | bytes 1114144 | tf_op jit(solution)/shard_map/all_to_all | solution.py:90
  125.6 0.7 copy.47
  126.3 0.5 convert_element_type.97
  126.7 0.7 gather_fusion.1
  127.4 0.7 gather_fusion.2
  128.1 0.7 gather_fusion.3
  128.7 0.7 gather_fusion.4
  129.4 0.7 gather_fusion.5
  130.0 0.7 gather_fusion.6
  130.7 0.7 gather_fusion.7
  131.3 0.7 gather_fusion.8
  132.0 1.0 add_convert_fusion
  (19 shorter events, 0.2 us)
Async XLA Ops:
  0.6 32.1 %copy-start = (bf16[4,64,2,2,128]{4,3,2,1,0:T(2,128)(2,1)S(1)}, bf16[4,64,2,2,128]{4,3,2,1,0:T(2,128)(2,1)}, u32[]{:S(2)}) copy-start(bf16[4,64,2,2,128]{4,3,2,1,0:T(2,128)(2,1)} %param.15) | copy-start | bytes 786436
  27.7 5.0 %copy-start.3 = (s32[1,4]{1,0:T(1,128)S(1)}, s32[1,4]{1,0:T(1,128)}, u32[]{:S(2)}) copy-start(s32[1,4]{1,0:T(1,128)} %param.16) | copy-start | bytes 52
  27.7 32.1 %all-to-all-start.1 = ((bf16[4,4,17,2048]{3,1,2,0:T(4,128)(2,1)}), bf16[4,4,17,2048]{3,1,2,0:T(4,128)(2,1)S(1)}, u32[]{:S(2)}, u32[]{:S(2)}) async-start(bf16[4,4,17,2048]{3,1,2,0:T(4,128)(2,1)} %copy.43), calls=%async_computation.1 | async-start | bytes 2228224 | tf_op jit(solution)/shard_map/all_to_all | solution.py:86
  74.7 4.0 %copy-start.2 = (bf16[1,32,128]{2,1,0:T(8,128)(2,1)S(1)}, bf16[1,32,128]{2,1,0:T(8,128)(2,1)}, u32[]{:S(2)}) copy-start(bf16[1,32,128]{2,1,0:T(8,128)(2,1)} %param.12) | copy-start | bytes 24580
  74.7 4.0 %copy-start.4 = (bf16[1,2,128]{2,1,0:T(2,128)(2,1)S(1)}, bf16[1,2,128]{2,1,0:T(2,128)(2,1)}, u32[]{:S(2)}) copy-start(bf16[1,2,128]{2,1,0:T(2,128)(2,1)} %param.13) | copy-start | bytes 1540
  74.7 4.6 %copy-start.5 = (bf16[1,2,128]{2,1,0:T(2,128)(2,1)S(1)}, bf16[1,2,128]{2,1,0:T(2,128)(2,1)}, u32[]{:S(2)}) copy-start(bf16[1,2,128]{2,1,0:T(2,128)(2,1)} %param.14) | copy-start | bytes 1540
  74.7 30.2 %all-to-all-start.2 = ((bf16[4,4,17,2048]{3,1,2,0:T(4,128)(2,1)}), bf16[4,4,17,2048]{3,1,2,0:T(4,128)(2,1)S(1)}, u32[]{:S(2)}, u32[]{:S(2)}) async-start(bf16[4,4,17,2048]{3,1,2,0:T(4,128)(2,1)} %copy.45), calls=%async_computation.2 | async-start | bytes 2228224 | tf_op jit(solution)/shard_map/all_to_all | solution.py:89
  106.8 3.7 %copy-start.1 = (f32[32,8]{0,1:T(8,128)S(1)}, f32[32,8]{0,1:T(8,128)}, u32[]{:S(2)}) copy-start(f32[32,8]{0,1:T(8,128)} %param.21) | copy-start | bytes 3076
  106.8 18.8 %all-to-all-start.3 = ((bf16[4,4,17,2048]{3,0,2,1:T(4,128)(2,1)}), bf16[4,4,17,2048]{3,0,2,1:T(4,128)(2,1)S(1)}, u32[]{:S(2)}, u32[]{:S(2)}) async-start(bf16[4,4,17,2048]{3,0,2,1:T(4,128)(2,1)} %copy.46), calls=%async_computation.3 | async-start | bytes 2228224 | tf_op jit(solution)/shard_map/all_to_all | solution.py:90
where the time goes:
time: 133 us
  waiting for transfers between devices  65.1 us (49%)
  blocking collectives  19.2 us (14%)
  local copies, waits for them, and re-layouts  17.3 us (13%)
  matrix products  14 us (11%)
  starting transfers between devices  12.3 us (9%)
  other arithmetic  3.53 us (3%)
  between operations  1.57 us (1%)
    all_to_all x1, waiting for transfers between devices, per_device(): lax.all_to_all(partial_rows, 'expert', split_axis=0, concat_axis=0, tiled...  25.7 us
    all_to_all x1, waiting for transfers between devices, per_device(): lax.all_to_all(in_rank, 'expert', split_axis=0, concat_axis=0, tiled=True)  25.2 us
    all_to_all x1, blocking collectives, per_device(): lax.all_to_all(copies, ('attn', 'tp'), split_axis=1, concat_axis=1, tiled...  19.2 us
    all_to_all x1, waiting for transfers between devices, per_device(): lax.all_to_all(returned, ('attn', 'tp'), split_axis=1, concat_axis=1, til...  14.2 us
    dot_general x1, matrix products, expert_part(): jnp.einsum('nd,gud->gnu', rows_in, weights_in, preferred_element_type=jnp...  6.69 us
    gather x8, local copies, waits for them, and re-layouts, per_device(): flat_home[placed[:, column]].astype(jnp.float32)  5.2 us
    all_to_all x1, starting transfers between devices, per_device(): lax.all_to_all(in_rank, 'expert', split_axis=0, concat_axis=0, tiled=True)  5 us
    dot_general x1, matrix products, expert_part(): jnp.dot(hidden, weights_out, preferred_element_type=jnp.float32)  4.74 us
  transfers between devices with their start and end apart: 3, of which 3 were waited for; matrix products, arithmetic and copies ran while one was open for 2% of the time, Pallas kernels for 0%

commit v1 on v0

--- a/solution.py
+++ b/solution.py
@@ -1,6 +1,10 @@
+import functools
+
 import jax
 import jax.numpy as jnp
 from jax import lax
+from jax.experimental import pallas as pl
+from jax.experimental.pallas import tpu as pltpu
 from jax.sharding import PartitionSpec as P
 
 TOP = 8
@@ -8,6 +12,355 @@
 
 
 epsilon = 1e-06
+MESH = pl.DeviceIdType.MESH
+K_PARTS = 4
+J_PARTS = 4
+UNIT_TILE = 512
+LOW = 64
+NT = (((1,), (1,)), ((), ()))
+
+
+def dot(a, b):
+    return jnp.dot(a, b, preferred_element_type=jnp.float32)
+
+
+def dot_nt(a, b):
+    return lax.dot_general(a, b, NT, preferred_element_type=jnp.float32)
+
+
+def attend_block(table, length, q, new_k, new_v, kv, out):
+    heads, size = q.shape
+    kv_heads = new_k.shape[0]
+    pages = table.shape[1]
+    columns = kv.shape[0]
+    page_len = columns // (pages * 2 * kv_heads)
+    per = heads // kv_heads
+    scale = size ** (-0.5)
+    col = lax.broadcasted_iota(jnp.int32, (heads, columns), 1)
+    head = lax.broadcasted_iota(jnp.int32, (heads, columns), 0)
+    token = lax.div(col, 2 * kv_heads)
+    inner = col - token * (2 * kv_heads)
+    page = lax.div(token, page_len)
+    slot = token - page * page_len
+    place = jnp.zeros_like(col)
+    for p in range(pages):
+        order = jnp.int32(0)
+        for j in range(pages):
+            order = order + jnp.where(table[0, j] == p, j, 0)
+        place = jnp.where(page == p, order * page_len + slot, place)
+    valid = (inner == lax.div(head, per)) & (place < length[0])
+    qv = q[...]
+    kvv = kv[...]
+    scores = jnp.where(valid, dot_nt(qv, kvv) * scale, -1e30)
+    row = lax.broadcasted_iota(jnp.int32, (heads, size), 0)
+    key = jnp.zeros((heads, size), jnp.float32)
+    value = jnp.zeros((heads, size), jnp.float32)
+    for g in range(kv_heads):
+        mine = lax.div(row, per) == g
+        key = jnp.where(mine, new_k[g : g + 1, :].astype(jnp.float32), key)
+        value = jnp.where(mine, new_v[g : g + 1, :].astype(jnp.float32), value)
+    own = jnp.sum(qv.astype(jnp.float32) * key, axis=1, keepdims=True) * scale
+    top = jnp.maximum(jnp.max(scores, axis=1, keepdims=True), own)
+    weights = jnp.where(valid, jnp.exp(scores - top), 0.0)
+    own_weight = jnp.exp(own - top)
+    total = jnp.sum(weights, axis=1, keepdims=True) + own_weight
+    probs = pltpu.roll(weights / total, kv_heads, 1).astype(jnp.bfloat16)
+    own_prob = (own_weight / total).astype(jnp.bfloat16).astype(jnp.float32)
+    out[...] = (dot(probs, kvv) + own_prob * value).astype(out.dtype)
+
+
+def layer_kernel(
+    table, length, q, new_k, new_v, kv_hbm, tokens, gain, ids, gates, win_hbm, wout_hbm,
+    attn_out, moe_out,
+    kv, win, wout, xg, mg, grid_in, grid_out, acc, hid, pj, ybuf, r1, s2, r2, s3, r3, keep,
+    local_sem, send_sem, gather_sem, r1_sem, r2_sem, r3_sem,
+):
+    z, x, c = lax.axis_index("expert"), lax.axis_index("attn"), lax.axis_index("tp")
+    ranks = lax.axis_size("expert")
+    rows, width = tokens.shape
+    devices = ranks * 4
+    total_rows = devices * rows
+    kc = width // K_PARTS
+    wj = width // J_PARTS
+    units = wout.shape[0]
+    slots = grid_in.shape[0]
+    choices = ids.shape[1]
+
+    def place_of(zz, xx, cc):
+        return (cc * 2 + xx) * ranks + zz
+
+    me = place_of(z, x, c)
+    expert = (z * 2 + x) * 2 + c
+    to_core, to_x = {"tp": 1 - c}, {"attn": 1 - x}
+    z_next = [lax.rem(z + d, ranks) for d in range(1, ranks)]
+    z_prev = [lax.rem(z + ranks - d, ranks) for d in range(1, ranks)]
+    peers = [to_core, to_x] + [{"expert": zz} for zz in z_next]
+
+    barrier = pltpu.get_barrier_semaphore()
+    for peer in peers:
+        pl.semaphore_signal(barrier, inc=1, device_id=peer, device_id_type=MESH)
+
+    local = []
+
+    def load(src, dst):
+        copy = pltpu.make_async_copy(src, dst, local_sem.at[len(local)])
+        copy.start()
+        local.append(copy)
+
+    load(kv_hbm, kv)
+    in_tiles = win.shape[0] // UNIT_TILE
+    for n in range(in_tiles):
+        part = pl.ds(n * UNIT_TILE, UNIT_TILE)
+        load(win_hbm.at[part], win.at[part])
+    for n in range(units // UNIT_TILE):
+        part = pl.ds(n * UNIT_TILE, UNIT_TILE)
+        load(wout_hbm.at[part], wout.at[part])
+
+    share = gates[...] / jnp.sum(gates[...], axis=1, keepdims=True)
+    high = share.astype(jnp.bfloat16).astype(jnp.float32)
+    low = share - high
+    lane = lax.broadcasted_iota(jnp.int32, (rows, 2 * LOW), 1)
+    meta = jnp.zeros((rows, 2 * LOW), jnp.float32)
+    chosen = ids[...]
+    for k in range(choices):
+        one = chosen[:, k : k + 1]
+        meta = jnp.where(lane == one, high[:, k : k + 1], meta)
+        meta = jnp.where(lane == one + LOW, low[:, k : k + 1], meta)
+    mg[me] = meta.astype(jnp.bfloat16)
+    floats = tokens[...].astype(jnp.float32)
+    normed = floats * lax.rsqrt(jnp.mean(floats * floats, axis=1, keepdims=True) + epsilon)
+    normed = (normed * gain[...]).astype(jnp.bfloat16)
+    for k in range(K_PARTS):
+        xg[k, me] = normed[:, k * kc : (k + 1) * kc]
+
+    pl.semaphore_wait(barrier, len(peers))
+    sent = []
+
+    def push(src, dst, recv, peer):
+        copy = pltpu.make_async_remote_copy(
+            src_ref=src, dst_ref=dst, send_sem=send_sem.at[len(sent)], recv_sem=recv,
+            device_id=peer, device_id_type=MESH,
+        )
+        copy.start()
+        sent.append(copy)
+
+    def arrived(ref, recv):
+        pltpu.make_async_remote_copy(
+            src_ref=ref, dst_ref=ref, send_sem=send_sem.at[0], recv_sem=recv,
+            device_id=to_core, device_id_type=MESH,
+        ).wait_recv()
+
+    def block(k, at):
+        return mg.at[at] if k == 0 else xg.at[k - 1, at]
+
+    def give(k, at, peer):
+        push(block(k, at), block(k, at), gather_sem.at[k, at], peer)
+
+    def take(k, at):
+        arrived(block(k, at), gather_sem.at[k, at])
+
+    def own_out(k):
+        give(k, me, to_x)
+        for zz in z_next:
+            give(k, me, {"expert": zz})
+        give(k, me, to_core)
+
+    def along_z(k):
+        for zz in z_prev:
+            at = place_of(zz, x, c)
+            take(k, at)
+            give(k, at, to_x)
+            give(k, at, to_core)
+
+    def along_x(k):
+        for zz in [z] + z_prev:
+            at = place_of(zz, 1 - x, c)
+            take(k, at)
+            give(k, at, to_core)
+
+    def along_core(k):
+        for xx in (x, 1 - x):
+            for zz in [z] + z_prev:
+                take(k, place_of(zz, xx, 1 - c))
+
+    for k in range(K_PARTS + 1):
+        own_out(k)
+    local[0].wait()
+    attend_block(table, length, q, new_k, new_v, kv, attn_out)
+    r_row = lax.broadcasted_iota(jnp.int32, (total_rows, total_rows), 0)
+    r_col = lax.broadcasted_iota(jnp.int32, (total_rows, total_rows), 1)
+    before = jnp.where(r_row > r_col, 1.0, 0.0).astype(jnp.bfloat16)
+    after = jnp.where(r_row < r_col, 1.0, 0.0).astype(jnp.bfloat16)
+    pj[...] = jnp.zeros_like(pj)
+    along_z(0)
+    along_z(1)
+    along_x(0)
+    along_core(0)
+
+    routes = mg[...].reshape(total_rows, 2 * LOW)
+    named = jnp.where(routes.astype(jnp.float32) > 0.0, 1.0, 0.0)
+    lanes = lax.broadcasted_iota(jnp.int32, (total_rows, 2 * LOW), 1)
+    named = jnp.where(lanes == expert, named, 0.0)
+    named_b = named.astype(jnp.bfloat16)
+    m_col = jnp.sum(named, axis=1, keepdims=True)
+    at_col = jnp.sum(dot(before, named_b), axis=1, keepdims=True)
+    ones = jnp.ones((16, 2 * LOW), jnp.bfloat16)
+    m_row = dot_nt(ones, named_b)
+    at_row = dot(m_row.astype(jnp.bfloat16), after)
+    s_row = lax.broadcasted_iota(jnp.int32, (slots, total_rows), 0).astype(jnp.float32)
+    grid_in[...] = jnp.where(
+        (s_row == at_row[0:1, :]) & (m_row[0:1, :] > 0.5), 1.0, 0.0
+    ).astype(jnp.bfloat16)
+    s_col = lax.broadcasted_iota(jnp.int32, grid_out.shape, 1).astype(jnp.float32)
+    grid_out[...] = jnp.where((s_col == at_col) & (m_col > 0.5), 1.0, 0.0).astype(jnp.bfloat16)
+    picked = dot(grid_in[...], routes)
+    p_lane = lax.broadcasted_iota(jnp.int32, (slots, 2 * LOW), 1)
+    slot_share = jnp.sum(
+        jnp.where((p_lane == expert) | (p_lane == expert + LOW), picked, 0.0), axis=1, keepdims=True
+    )
+    along_x(1)
+
+    for copy in local[1:]:
+        copy.wait()
+    for k in range(K_PARTS):
+        if k + 1 < K_PARTS:
+            along_z(k + 2)
+        along_core(k + 1)
+        rows_in = dot(grid_in[...], xg[k].reshape(total_rows, kc)).astype(jnp.bfloat16)
+
+        def tile(n, _, k=k, rows_in=rows_in):
+            start = pl.multiple_of(n * UNIT_TILE, UNIT_TILE)
+            product = dot_nt(rows_in, win[pl.ds(start, UNIT_TILE), k * kc : (k + 1) * kc])
+            acc[n] = product if k == 0 else acc[n] + product
+            return 0
+
+        lax.fori_loop(0, in_tiles, tile, 0)
+        if k + 1 < K_PARTS:
+            along_x(k + 2)
+
+    for n in range(in_tiles // 2):
+        gate = acc[n]
+        hid[:, n * UNIT_TILE : (n + 1) * UNIT_TILE] = (
+            gate / (1.0 + jnp.exp(-gate)) * acc[n + in_tiles // 2]
+        ).astype(jnp.bfloat16)
+
+    half = grid_out.shape[0] // 2
+
+    def first(j):
+        part = dot(hid[...], wout[:, j * wj : (j + 1) * wj]) * slot_share
+        pj[0:slots, :] = part.astype(jnp.bfloat16)
+        for cc in (1 - c, c):
+            spread = dot(grid_out[pl.ds(pl.multiple_of(cc * half, half), half), :], pj[...])
+            ybuf[j, cc] = spread.astype(jnp.bfloat16).reshape(2, half // 2, wj)
+            if cc is not c:
+                push(ybuf.at[j, cc], r1.at[j], r1_sem.at[j], to_core)
+
+    def second(j):
+        arrived(r1.at[j], r1_sem.at[j])
+        s2[j] = (
+            ybuf[j, c, 1 - x].astype(jnp.float32) + r1[j, 1 - x].astype(jnp.float32)
+        ).astype(jnp.bfloat16)
+        push(s2.at[j], r2.at[j], r2_sem.at[j], to_x)
+
+    def third(j):
+        arrived(r2.at[j], r2_sem.at[j])
+        for zz in z_next + [z]:
+            part = pl.ds(pl.multiple_of(zz * rows, rows), rows)
+            value = (
+                ybuf[j, c, x, part, :].astype(jnp.float32)
+                + r1[j, x, part, :].astype(jnp.float32)
+                + r2[j, part, :].astype(jnp.float32)
+            )
+            if zz is z:
+                keep[j] = value
+            else:
+                s3[j, zz] = value.astype(jnp.bfloat16)
+                push(s3.at[j, zz], r3.at[j, z], r3_sem.at[j, z], {"expert": zz})
+
+    def fourth(j):
+        value = keep[j]
+        for zz in z_prev:
+            arrived(r3.at[j, zz], r3_sem.at[j, zz])
+            value = value + r3[j, zz].astype(jnp.float32)
+        moe_out[:, j * wj : (j + 1) * wj] = value.astype(moe_out.dtype)
+
+    for j in range(J_PARTS):
+        first(j)
+        if j:
+            second(j - 1)
+    second(J_PARTS - 1)
+    for j in range(J_PARTS):
+        third(j)
+        if j:
+            fourth(j - 1)
+    fourth(J_PARTS - 1)
+    for copy in sent:
+        copy.wait_send()
+
+
+def fused_layer(
+    queries, new_keys, new_values, kv_cache, block_tables, cache_lengths,
+    tokens, gain, expert_ids, gate_weights, w_in, w_out,
+):
+    rows, width = tokens.shape
+    ranks = lax.axis_size("expert")
+    devices = 4 * ranks
+    experts = devices
+    most = max(2, rows * TOP // experts + 1)
+    slots = -(-most * devices // 16) * 16
+    padded = -(-slots // 128) * 128
+    units = w_out.shape[1]
+    total = devices * rows
+    kc, wj = width // K_PARTS, width // J_PARTS
+    heads, size = queries.shape[1:]
+    bf, f32 = jnp.bfloat16, jnp.float32
+    kv = kv_cache.reshape(-1, size)
+    sends = 15 * (K_PARTS + 1) + (2 + ranks - 1) * J_PARTS
+    vmem = pl.BlockSpec(memory_space=pltpu.VMEM)
+    smem = pl.BlockSpec(memory_space=pltpu.SMEM)
+    anyw = pl.BlockSpec(memory_space=pl.ANY)
+    attn_out, moe_out = pl.pallas_call(
+        layer_kernel,
+        out_shape=(
+            jax.ShapeDtypeStruct((heads, size), bf),
+            jax.ShapeDtypeStruct((rows, width), bf),
+        ),
+        in_specs=[smem, smem, vmem, vmem, vmem, anyw, vmem, vmem, vmem, vmem, anyw, anyw],
+        out_specs=(vmem, vmem),
+        scratch_shapes=[
+            pltpu.VMEM(kv.shape, bf),
+            pltpu.VMEM((2 * units, width), bf),
+            pltpu.VMEM((units, width), bf),
+            pltpu.VMEM((K_PARTS, devices, rows, kc), bf),
+            pltpu.VMEM((devices, rows, 2 * LOW), bf),
+            pltpu.VMEM((slots, total), bf),
+            pltpu.VMEM((total, padded), bf),
+            pltpu.VMEM((2 * units // UNIT_TILE, slots, UNIT_TILE), f32),
+            pltpu.VMEM((slots, units), bf),
+            pltpu.VMEM((padded, wj), bf),
+            pltpu.VMEM((J_PARTS, 2, 2, total // 4, wj), bf),
+            pltpu.VMEM((J_PARTS, 2, total // 4, wj), bf),
+            pltpu.VMEM((J_PARTS, total // 4, wj), bf),
+            pltpu.VMEM((J_PARTS, total // 4, wj), bf),
+            pltpu.VMEM((J_PARTS, ranks, rows, wj), bf),
+            pltpu.VMEM((J_PARTS, ranks, rows, wj), bf),
+            pltpu.VMEM((J_PARTS, rows, wj), f32),
+            pltpu.SemaphoreType.DMA((1 + 3 * units // UNIT_TILE,)),
+            pltpu.SemaphoreType.DMA((sends,)),
+            pltpu.SemaphoreType.DMA((K_PARTS + 1, devices)),
+            pltpu.SemaphoreType.DMA((J_PARTS,)),
+            pltpu.SemaphoreType.DMA((J_PARTS,)),
+            pltpu.SemaphoreType.DMA((J_PARTS, ranks)),
+        ],
+        compiler_params=pltpu.CompilerParams(
+            collective_id=0, has_side_effects=True, vmem_limit_bytes=56 * 1024 * 1024
+        ),
+    )(
+        block_tables, cache_lengths, queries[0], new_keys[0], new_values[0], kv,
+        tokens, gain.reshape(1, width), expert_ids, gate_weights,
+        w_in.reshape(2 * units, width), w_out.reshape(units, width),
+    )
+    return (attn_out.reshape(1, heads, size), moe_out)
 
 
 def attend(queries, new_keys, new_values, kv_cache, block_tables, cache_lengths):
@@ -59,6 +412,13 @@
     w_in,
     w_out,
 ):
+    ranks, cores = lax.axis_size("expert"), lax.axis_size("tp")
+    fits = ranks * 4 * tokens.shape[0] <= 512 and queries.shape[0] == 1
+    if lax.axis_size("attn") == 2 and cores == 2 and fits:
+        return fused_layer(
+            queries, new_keys, new_values, kv_cache, block_tables, cache_lengths,
+            tokens, gain, expert_ids, gate_weights, w_in, w_out,
+        )
     attn_out = attend(queries, new_keys, new_values, kv_cache, block_tables, cache_lengths)
     rows, width = tokens.shape
     ranks = lax.axis_size("expert")

time: 133 us -> 61.8 us (0.46)
  waiting for transfers between devices: 65.1 us -> 0 us
  Pallas kernels: 0 us -> 54.6 us
  blocking collectives: 19.2 us -> 0 us
  matrix products: 14 us -> 0 us
  starting transfers between devices: 12.3 us -> 0 us
  local copies, waits for them, and re-layouts: 17.3 us -> 5.59 us
  other arithmetic: 3.53 us -> 0 us
    all_to_all x3 -> x0, waiting for transfers between devices: 65.1 us -> none  [the longest x1 25.7 us: per_device(): lax.all_to_all(partial_rows, 'expert', split_axis=0, concat_axis=0, tiled...]
    pallas_call x0 -> x1, Pallas kernels: none -> 54.6 us  [fused_layer(): pl.pallas_call(layer_kernel, out_shape=(jax.ShapeDtypeStruct((heads, size...]
    all_to_all x1 -> x0, blocking collectives: 19.2 us -> none  [per_device(): lax.all_to_all(copies, ('attn', 'tp'), split_axis=1, concat_axis=1, tiled...]
    dot_general x6 -> x0, matrix products: 14 us -> none  [the longest x1 6.69 us: expert_part(): jnp.einsum('nd,gud->gnu', rows_in, weights_in, preferred_element_type=jnp...]
    all_to_all x3 -> x0, starting transfers between devices: 12.3 us -> none  [the longest x1 5 us: per_device(): lax.all_to_all(in_rank, 'expert', split_axis=0, concat_axis=0, tiled=True)]
    gather x10 -> x0, local copies, waits for them, and re-layouts: 6.32 us -> none  [the longest x8 5.2 us: per_device(): flat_home[placed[:, column]].astype(jnp.float32)]
    all_to_all x4 -> x0, local copies, waits for them, and re-layouts: 5.02 us -> none  [the longest x1 1.85 us: per_device(): lax.all_to_all(partial_rows, 'expert', split_axis=0, concat_axis=0, tiled...]
    unnamed x13 -> x4, local copies, waits for them, and re-layouts: 0.83 us -> 5.59 us
  transfers between devices with their start and end apart: 3 -> 0, of which waited for: 3 -> 0; matrix products, arithmetic and copies ran while one was open for 2% -> 0% of each run, Pallas kernels for 0% -> 0%
where the time goes in v1:
time: 61.8 us; the launch traced here: 61.5 us
  Pallas kernels  54.6 us (88%)
  local copies, waits for them, and re-layouts  5.59 us (9%)
  between operations  1.29 us (2%)
    pallas_call x1, Pallas kernels, fused_layer(): pl.pallas_call(layer_kernel, out_shape=(jax.ShapeDtypeStruct((heads, size...  54.6 us
    unnamed x4, local copies, waits for them, and re-layouts  5.59 us

profile of v1, /device:TPU:0, one launch (start us, length us, event | category | flops | bytes accessed | tf_op | source)
XLA Modules:
  0.0 61.5 jit_solution(5324168582256790707)
XLA Ops:
  1.3 1.4 %copy.14.ids = s32[32,8]{1,0:T(8,128)} copy(s32[32,8]{0,1:T(8,128)} %param.20) | data formatting | bytes 2048 | tf_op args[8]
  2.6 1.4 %copy.15.gates = f32[32,8]{1,0:T(8,128)} copy(f32[32,8]{0,1:T(8,128)} %param.21) | data formatting | bytes 2048 | tf_op args[9]
  4.0 54.6 %shard_map.131 = (bf16[32,128]{1,0:T(8,128)(2,1)}, bf16[32,2048]{1,0:T(8,128)(2,1)}) custom-call(s32[1,4]{1,0:T(1,128)} %table.1, s32[1]{0:T(128)S(6)} %copy.18.length, bf16[32,128]{1,0:T(8,128)(2,1)} %bitcast.11, bf16[2,128]{1,0:T(2,128)(2,1)} %bitcast.14, bf16[2,128]{1,0:T(2,128)(2,1)} %bitcast.15, bf16[1024,128]{1,0:T(8,128)(2,1)} %bitcast.10, ...), custom_call_target="tpu_custom_call" | custom-call | tf_op jit(solution)/shard_map/pallas_call | solution.py:322
  58.6 1.3 %copy.19 = bf16[1,32,128]{2,1,0:T(8,128)(2,1)} copy(bf16[1,32,128]{2,1,0:T(8,128)(2,1)} %bitcast.13) | data formatting | bytes 16384
  59.9 1.6 %copy.20 = bf16[32,2048]{1,0:T(8,128)(2,1)} copy(bf16[32,2048]{1,0:T(8,128)(2,1)} %get-tuple-element.9) | data formatting | bytes 262144

commit v2 on v1

--- a/solution.py
+++ b/solution.py
@@ -13,9 +13,9 @@
 
 epsilon = 1e-06
 MESH = pl.DeviceIdType.MESH
-K_PARTS = 4
+K_PARTS = 2
 J_PARTS = 4
-UNIT_TILE = 512
+UNIT_TILE = 768
 LOW = 64
 NT = (((1,), (1,)), ((), ()))
 
@@ -84,7 +84,7 @@
     wj = width // J_PARTS
     units = wout.shape[0]
     slots = grid_in.shape[0]
-    choices = ids.shape[1]
+    choices = ids.shape[0]
 
     def place_of(zz, xx, cc):
         return (cc * 2 + xx) * ranks + zz
@@ -116,17 +116,21 @@
         part = pl.ds(n * UNIT_TILE, UNIT_TILE)
         load(wout_hbm.at[part], wout.at[part])
 
-    share = gates[...] / jnp.sum(gates[...], axis=1, keepdims=True)
+    share = gates[...] / jnp.sum(gates[...], axis=0, keepdims=True)
     high = share.astype(jnp.bfloat16).astype(jnp.float32)
     low = share - high
-    lane = lax.broadcasted_iota(jnp.int32, (rows, 2 * LOW), 1)
-    meta = jnp.zeros((rows, 2 * LOW), jnp.float32)
+    name = lax.broadcasted_iota(jnp.int32, (2 * LOW, rows), 0)
+    meta = jnp.zeros((2 * LOW, rows), jnp.float32)
     chosen = ids[...]
     for k in range(choices):
-        one = chosen[:, k : k + 1]
-        meta = jnp.where(lane == one, high[:, k : k + 1], meta)
-        meta = jnp.where(lane == one + LOW, low[:, k : k + 1], meta)
-    mg[me] = meta.astype(jnp.bfloat16)
+        one = chosen[k : k + 1, :]
+        meta = jnp.where(name == one, high[k : k + 1, :], meta)
+        meta = jnp.where(name == one + LOW, low[k : k + 1, :], meta)
+    same = lax.broadcasted_iota(jnp.int32, (rows, rows), 0) == lax.broadcasted_iota(
+        jnp.int32, (rows, rows), 1
+    )
+    unit = jnp.where(same, 1.0, 0.0).astype(jnp.bfloat16)
+    mg[me] = dot_nt(unit, meta.astype(jnp.bfloat16)).astype(jnp.bfloat16)
     floats = tokens[...].astype(jnp.float32)
     normed = floats * lax.rsqrt(jnp.mean(floats * floats, axis=1, keepdims=True) + epsilon)
     normed = (normed * gain[...]).astype(jnp.bfloat16)
@@ -134,15 +138,17 @@
         xg[k, me] = normed[:, k * kc : (k + 1) * kc]
 
     pl.semaphore_wait(barrier, len(peers))
-    sent = []
+    sent, across, used = [], [], [0]
 
     def push(src, dst, recv, peer):
         copy = pltpu.make_async_remote_copy(
-            src_ref=src, dst_ref=dst, send_sem=send_sem.at[len(sent)], recv_sem=recv,
+            src_ref=src, dst_ref=dst, send_sem=send_sem.at[used[0]], recv_sem=recv,
             device_id=peer, device_id_type=MESH,
         )
         copy.start()
+        used[0] += 1
         sent.append(copy)
+        return copy
 
     def arrived(ref, recv):
         pltpu.make_async_remote_copy(
@@ -159,16 +165,19 @@
     def take(k, at):
         arrived(block(k, at), gather_sem.at[k, at])
 
-    def own_out(k):
+    def own_near(k):
         give(k, me, to_x)
-        for zz in z_next:
-            give(k, me, {"expert": zz})
         give(k, me, to_core)
 
+    def own_far(k, i):
+        give(k, me, {"expert": z_next[i]})
+
     def along_z(k):
-        for zz in z_prev:
+        for i, zz in enumerate(z_prev):
             at = place_of(zz, x, c)
             take(k, at)
+            if k and k < K_PARTS:
+                own_far(k + 1, i)
             give(k, at, to_x)
             give(k, at, to_core)
 
@@ -183,8 +192,11 @@
             for zz in [z] + z_prev:
                 take(k, place_of(zz, xx, 1 - c))
 
+    for k in range(2):
+        for i in range(ranks - 1):
+            own_far(k, i)
     for k in range(K_PARTS + 1):
-        own_out(k)
+        own_near(k)
     local[0].wait()
     attend_block(table, length, q, new_k, new_v, kv, attn_out)
     r_row = lax.broadcasted_iota(jnp.int32, (total_rows, total_rows), 0)
@@ -260,7 +272,9 @@
         s2[j] = (
             ybuf[j, c, 1 - x].astype(jnp.float32) + r1[j, 1 - x].astype(jnp.float32)
         ).astype(jnp.bfloat16)
-        push(s2.at[j], r2.at[j], r2_sem.at[j], to_x)
+        if j:
+            across[j - 1].wait_send()
+        across.append(push(s2.at[j], r2.at[j], r2_sem.at[j], to_x))
 
     def third(j):
         arrived(r2.at[j], r2_sem.at[j])
@@ -284,18 +298,13 @@
             value = value + r3[j, zz].astype(jnp.float32)
         moe_out[:, j * wj : (j + 1) * wj] = value.astype(moe_out.dtype)
 
-    for j in range(J_PARTS):
-        first(j)
-        if j:
-            second(j - 1)
-    second(J_PARTS - 1)
-    for j in range(J_PARTS):
-        third(j)
-        if j:
-            fourth(j - 1)
-    fourth(J_PARTS - 1)
+    for step in range(J_PARTS + 4):
+        for lag, stage in ((0, first), (1, second), (2, third), (4, fourth)):
+            if 0 <= step - lag < J_PARTS:
+                stage(step - lag)
     for copy in sent:
-        copy.wait_send()
+        if not any(copy is early for early in across[:-1]):
+            copy.wait_send()
 
 
 def fused_layer(
@@ -357,7 +366,7 @@
         ),
     )(
         block_tables, cache_lengths, queries[0], new_keys[0], new_values[0], kv,
-        tokens, gain.reshape(1, width), expert_ids, gate_weights,
+        tokens, gain.reshape(1, width), expert_ids.T, gate_weights.T,
         w_in.reshape(2 * units, width), w_out.reshape(units, width),
     )
     return (attn_out.reshape(1, heads, size), moe_out)

time: 61.8 us -> 55.9 us (0.905)
  Pallas kernels: 54.6 us -> 51.5 us
  local copies, waits for them, and re-layouts: 5.59 us -> 2.86 us
    pallas_call x1, Pallas kernels: 54.6 us -> 51.5 us  [fused_layer(): pl.pallas_call(layer_kernel, out_shape=(jax.ShapeDtypeStruct((heads, size...]
    unnamed x4 -> x2, local copies, waits for them, and re-layouts: 5.59 us -> 2.86 us
where the time goes in v2:
time: 55.9 us; the launch traced here: 55.7 us
  Pallas kernels  51.5 us (92%)
  local copies, waits for them, and re-layouts  2.86 us (5%)
  between operations  1.29 us (2%)
    pallas_call x1, Pallas kernels, fused_layer(): pl.pallas_call(layer_kernel, out_shape=(jax.ShapeDtypeStruct((heads, size...  51.5 us
    unnamed x2, local copies, waits for them, and re-layouts  2.86 us

profile of v2, /device:TPU:0, one launch (start us, length us, event | category | flops | bytes accessed | tf_op | source)
XLA Modules:
  0.0 55.7 jit_solution(15392447849902042042)
XLA Ops:
  1.3 51.5 %shard_map.131 = (bf16[32,128]{1,0:T(8,128)(2,1)}, bf16[32,2048]{1,0:T(8,128)(2,1)}) custom-call(s32[1,4]{1,0:T(1,128)} %table.1, s32[1]{0:T(128)S(6)} %copy.16.length, bf16[32,128]{1,0:T(8,128)(2,1)} %bitcast.13, bf16[2,128]{1,0:T(2,128)(2,1)} %bitcast.18, bf16[2,128]{1,0:T(2,128)(2,1)} %bitcast.19, bf16[1024,128]{1,0:T(8,128)(2,1)} %bitcast.12, ...), custom_call_target="tpu_custom_call" | custom-call | tf_op jit(solution)/shard_map/pallas_call | solution.py:331
  52.8 1.3 %copy.17 = bf16[1,32,128]{2,1,0:T(8,128)(2,1)} copy(bf16[1,32,128]{2,1,0:T(8,128)(2,1)} %bitcast.15) | data formatting | bytes 16384
  54.1 1.6 %copy.18 = bf16[32,2048]{1,0:T(8,128)(2,1)} copy(bf16[32,2048]{1,0:T(8,128)(2,1)} %get-tuple-element.9) | data formatting | bytes 262144

commit v3 on v2

--- a/solution.py
+++ b/solution.py
@@ -230,13 +230,15 @@
     slot_share = jnp.sum(
         jnp.where((p_lane == expert) | (p_lane == expert + LOW), picked, 0.0), axis=1, keepdims=True
     )
+    if K_PARTS > 1:
+        along_z(2)
     along_x(1)
 
     for copy in local[1:]:
         copy.wait()
     for k in range(K_PARTS):
-        if k + 1 < K_PARTS:
-            along_z(k + 2)
+        if k + 2 < K_PARTS:
+            along_z(k + 3)
         along_core(k + 1)
         rows_in = dot(grid_in[...], xg[k].reshape(total_rows, kc)).astype(jnp.bfloat16)
 

time: 55.9 us -> 55.8 us (level)
  no operation moved by 1% of the time
where the time goes in v3:
time: 55.8 us; the launch traced here: 55.6 us
  Pallas kernels  51.5 us (92%)
  local copies, waits for them, and re-layouts  2.86 us (5%)
  between operations  1.29 us (2%)
    pallas_call x1, Pallas kernels, fused_layer(): pl.pallas_call(layer_kernel, out_shape=(jax.ShapeDtypeStruct((heads, size...  51.5 us
    unnamed x2, local copies, waits for them, and re-layouts  2.86 us

profile of v3, /device:TPU:0, one launch (start us, length us, event | category | flops | bytes accessed | tf_op | source)
XLA Modules:
  0.0 55.6 jit_solution(15979921554948870275)
XLA Ops:
  1.3 51.5 %shard_map.131 = (bf16[32,128]{1,0:T(8,128)(2,1)}, bf16[32,2048]{1,0:T(8,128)(2,1)}) custom-call(s32[1,4]{1,0:T(1,128)} %table.1, s32[1]{0:T(128)S(6)} %copy.16.length, bf16[32,128]{1,0:T(8,128)(2,1)} %bitcast.13, bf16[2,128]{1,0:T(2,128)(2,1)} %bitcast.18, bf16[2,128]{1,0:T(2,128)(2,1)} %bitcast.19, bf16[1024,128]{1,0:T(8,128)(2,1)} %bitcast.12, ...), custom_call_target="tpu_custom_call" | custom-call | tf_op jit(solution)/shard_map/pallas_call | solution.py:333
  52.8 1.3 %copy.17 = bf16[1,32,128]{2,1,0:T(8,128)(2,1)} copy(bf16[1,32,128]{2,1,0:T(8,128)(2,1)} %bitcast.15) | data formatting | bytes 16384
  54.1 1.6 %copy.18 = bf16[32,2048]{1,0:T(8,128)(2,1)} copy(bf16[32,2048]{1,0:T(8,128)(2,1)} %get-tuple-element.9) | data formatting | bytes 262144
